TPU v7x, 256 devices: a whole 4x4x8 slice. The times are simulated.
256 devices in a mesh: gossip: 16 (over z_lo, x, core), fsdp: 16 (over y, z_hi).
Axes of the slice: x: 4, y: 4, z: 8 (z_hi: 4, z_lo: 2; z = z_hi * 2 + z_lo), core: 2. Of those that a mesh axis runs over, the one named last changes fastest.
Arguments:
- step_index: int32 [1], replicated, may hold values from 0 to 63
- weights: float32 [16, 4096, 1024], P('gossip', 'fsdp'), may hold values from -0.09375 to 0.09375
- momentum: float32 [16, 4096, 1024], P('gossip', 'fsdp'), may hold values from -3 to 3
- second_moment: float32 [16, 4096, 1024], P('gossip', 'fsdp'), may hold values from 0.05 to 1
- gradients: bfloat16 [2, 16, 4096, 1024], P(None, 'gossip', 'fsdp'), may hold values from -6 to 6
- tokens: bfloat16 [16, 7168, 4096], P('gossip', 'fsdp'), may hold values from -6 to 6
Outputs:
- new_weights: float32 [16, 4096, 1024], P('gossip', 'fsdp')
- new_momentum: float32 [16, 4096, 1024], P('gossip', 'fsdp')
- new_second: float32 [16, 4096, 1024], P('gossip', 'fsdp')
- projected: float32 [16, 7168, 1024], P('gossip', 'fsdp')
All inputs are finite; a program needn't handle non-finite values.
Results may differ from a plain program's by a relative error of at most 0.0003.
The roundings to bfloat16 on the way count: a program that leaves them out, or rounds other values in their place, can miss the bound.
Values may be sent and summed in bfloat16 or wider, within the bound.
A program may use at most 128 MiB of HBM per device.

v0:
```python
from functools import partial

import jax
import jax.numpy as jnp
from jax import lax
from jax.sharding import PartitionSpec as P

STEPS = 2


BETA_ONE = 0.9
BETA_TWO = 0.95
RATE = 0.003
DECAY = 0.1
EPSILON = 1e-08


def from_partner(block, axis, apart):
    count = lax.axis_size(axis)
    route = []
    for low in range(count):
        high = low | 1 << apart
        if high != low and high < count:
            route += [(low, high), (high, low)]
    return lax.ppermute(block, axis, route)


def finish_step(avg_w, moment, second, count):
    corr_one = 1.0 - jnp.power(jnp.float32(BETA_ONE), count)
    corr_two = 1.0 - jnp.power(jnp.float32(BETA_TWO), count)
    update = moment / corr_one / (jnp.sqrt(second / corr_two) + EPSILON) + DECAY * avg_w
    return avg_w - RATE * update


def update_block(weights, momentum, second, grad, far_w, far_m, count):
    gradf = grad.astype(jnp.float32)
    avg_w = 0.5 * (weights + far_w)
    avg_m = 0.5 * (momentum + far_m)
    moment = BETA_ONE * avg_m + (1.0 - BETA_ONE) * gradf
    second = BETA_TWO * second + (1.0 - BETA_TWO) * gradf * gradf
    return (finish_step(avg_w, moment, second, count), moment, second)


def step_whole(level, operands):
    weights, momentum, second, grad, count = operands
    far_w, far_m = from_partner((weights, momentum), "gossip", level)
    return update_block(weights, momentum, second, grad, far_w, far_m, count)


def per_device(step_index, weights, momentum, second_moment, gradients, tokens):
    levels = lax.axis_size("gossip").bit_length() - 1
    branches = [partial(step_whole, level) for level in range(levels)]
    for step in range(STEPS):
        now = step_index[0] + step
        bit_now = jnp.mod(now, levels)
        count = (now + 1).astype(jnp.float32)
        weights, momentum, second_moment = lax.switch(
            bit_now, branches, (weights, momentum, second_moment, gradients[step], count)
        )
    rounded = weights[0].astype(jnp.bfloat16)
    rows = tokens[0]
    whole = lax.all_gather(rounded, "fsdp", axis=0, tiled=True)
    total = jnp.dot(rows, whole, preferred_element_type=jnp.float32)
    return (weights, momentum, second_moment, total[None])


def solution(mesh):
    placed = (
        P(),
        P("gossip", "fsdp", None),
        P("gossip", "fsdp", None),
        P("gossip", "fsdp", None),
        P(None, "gossip", "fsdp", None),
        P("gossip", "fsdp", None),
    )
    return jax.shard_map(
        per_device,
        mesh=mesh,
        in_specs=placed,
        out_specs=(
            P("gossip", "fsdp", None),
            P("gossip", "fsdp", None),
            P("gossip", "fsdp", None),
            P("gossip", "fsdp", None),
        ),
        check_vma=False,
    )
```

profile of v0, /device:TPU:35, one launch (start us, length us, event | category | flops | bytes accessed | tf_op | source)
XLA Modules:
  0.0 258.2 jit_solution(17139195857605667928)
XLA Ops:
  7.2 0.0 all-gather.3.cloned.1.call-start
  7.9 2.2 slice_bitcast_fusion
  10.1 51.3 %conditional.2 = (f32[1,256,1024]{2,1,0:T(8,128)S(1)}, f32[1,256,1024]{2,1,0:T(8,128)S(1)}, f32[1,256,1024]{2,1,0:T(8,128)S(1)}) conditional(s32[]{:T(128)} %clamp.7, (f32[1,256,1024]{2,1,0:T(8,128)}, f32[1,256,1024]{2,1,0:T(8,128)}, bf16[1,256,1024]{2,1,0:T(8,128)(2,1)}, f32[]{:T(128)}, ...), branch_computations={%region_0.1_spmd, %region_1.2_spmd, %region_2.3_spmd, %region_3.4_... | conditional | flops 4980738 | bytes 25690328 | solution.py:57
  10.1 0.3 collective-permute-start.10
  10.4 1.2 collective-permute-start.11
  11.7 22.7 %collective-permute-done.10 = f32[1,256,1024]{2,1,0:T(8,128)S(1)} collective-permute-done((f32[1,256,1024]{2,1,0:T(8,128)}, f32[1,256,1024]{2,1,0:T(8,128)S(1)}, u32[]{:S(2)}, u32[]{:S(2)}) %collective-permute-start.10) | collective-permute-done | bytes 1048608 | tf_op jit(solution)/shard_map/cond/branch_1_fun/ppermute | solution.py:25
  34.4 22.5 %collective-permute-done.11 = f32[1,256,1024]{2,1,0:T(8,128)S(1)} collective-permute-done((f32[1,256,1024]{2,1,0:T(8,128)}, f32[1,256,1024]{2,1,0:T(8,128)S(1)}, u32[]{:S(2)}, u32[]{:S(2)}) %collective-permute-start.11) | collective-permute-done | bytes 1048608 | tf_op jit(solution)/shard_map/cond/branch_1_fun/ppermute | solution.py:25
  56.8 1.0 copy-done.7
  57.8 3.6 %multiply_subtract_fusion.1 = (f32[1,256,1024]{2,1,0:T(8,128)S(1)}, f32[1,256,1024]{2,1,0:T(8,128)S(1)}, f32[1,256,1024]{2,1,0:T(8,128)S(1)}) fusion(f32[1,256,1024]{2,1,0:T(8,128)} %get-tuple-element.99, f32[1,256,1024]{2,1,0:T(8,128)} %copy-done.3, f32[]{:T(128)S(6)} %sub.43, f32[]{:T(128)S(6)} %sub.42, bf16[1,256,1024]{2,1,0:T(8,128)(2,1)} %get-tuple-element.101, ...), kind=kLoop, calls=%fused_computation.9 | loop fusion | flops 4980736 | bytes 8912904 | tf_op jit(solution)/shard_map/cond/branch_1_fun/sub | solution.py:32
  61.4 54.7 %conditional.3 = (f32[1,256,1024]{2,1,0:T(8,128)}, f32[1,256,1024]{2,1,0:T(8,128)S(1)}, f32[1,256,1024]{2,1,0:T(8,128)}, f32[1,256,1024]{2,1,0:T(8,128)S(1)}, f3...) conditional(s32[]{:T(128)} %clamp.6, ...), branch_computations={%region_4.5_spmd, %region_5.6_spmd, %region_6.7_spmd, %region_7.8_... | conditional | flops 2621440 | bytes 25690344 | solution.py:57
  61.6 1.9 collective-permute-start.4
  63.5 1.2 collective-permute-start.5
  64.7 21.7 %collective-permute-done.4 = f32[1,256,1024]{2,1,0:T(8,128)} collective-permute-done((f32[1,256,1024]{2,1,0:T(8,128)S(1)}, f32[1,256,1024]{2,1,0:T(8,128)}, u32[]{:S(2)}, u32[]{:S(2)}) %collective-permute-start.4) | collective-permute-done | bytes 1048608 | tf_op jit(solution)/shard_map/cond/branch_2_fun/ppermute | solution.py:25
  86.4 3.1 %fusion.13 = (f32[1,256,1024]{2,1,0:T(8,128)}, f32[1,256,1024]{2,1,0:T(8,128)}) fusion(bf16[1,256,1024]{2,1,0:T(8,128)(2,1)} %get-tuple-element.125, f32[1,256,1024]{2,1,0:T(8,128)S(1)} %get-tuple-element.126, f32[1,256,1024]{2,1,0:T(8,128)S(1)} %get-tuple-element.124, f32[1,256,1024]{2,1,0:T(8,128)} %collective-permute-done.4), kind=kLoop, calls=%fused_computation.31 | loop fusion | flops 2359296 | bytes 5767168 | tf_op jit(solution)/shard_map/cond/branch_2_fun/add | solution.py:40
  89.5 19.4 %collective-permute-done.5 = f32[1,256,1024]{2,1,0:T(8,128)} collective-permute-done((f32[1,256,1024]{2,1,0:T(8,128)S(1)}, f32[1,256,1024]{2,1,0:T(8,128)}, u32[]{:S(2)}, u32[]{:S(2)}) %collective-permute-start.5) | collective-permute-done | bytes 1048608 | tf_op jit(solution)/shard_map/cond/branch_2_fun/ppermute | solution.py:25
  108.9 2.3 add.139
  111.2 1.2 copy.115
  112.4 1.2 copy.116
  113.7 1.2 copy.117
  114.9 1.1 broadcast.148.clone
  116.0 0.1 broadcast.148
  116.2 3.7 %fusion.32 = (bf16[1,256,1024]{2,1,0:T(8,128)(2,1)}, f32[1,256,1024]{2,1,0:T(8,128)}) fusion(f32[1,256,1024]{2,1,0:T(8,128)S(1)} %get-tuple-element.151, f32[1,256,1024]{2,1,0:T(8,128)} %get-tuple-element.157, f32[1,256,1024]{2,1,0:T(8,128)S(1)} %get-tuple-element.145, f32[1,256,1024]{2,1,0:T(8,128)S(1)} %get-tuple-element.146, f32[]{:T(128)S(6)} %sub.58, ...), kind=kLoop, calls=%fused_computation.43 | loop fusion | flops 2621440 | bytes 5767176 | tf_op jit(solution)/shard_map/convert_element_type | solution.py:60
  119.9 121.7 %all-gather.3.cloned.1.call-done = bf16[1,4096,1024]{2,1,0:T(8,128)(2,1)} async-done(((bf16[1,256,1024]{2,1,0:T(8,128)(2,1)}), bf16[1,4096,1024]{2,1,0:T(8,128)(2,1)}) %all-gather.3.cloned.1.call-update) | async-done | bytes 8388624 | tf_op jit(solution)/shard_map/all_gather | solution.py:62
  241.7 9.7 %fusion.19 = f32[1,448,1024]{2,1,0:T(8,128)} fusion(bf16[1,4096,1024]{2,1,0:T(8,128)(2,1)} %all-gather.3.cloned.1.call-done, bf16[1,448,4096]{2,1,0:T(8,128)(2,1)} %param.19), kind=kOutput, calls=%fused_computation.39 | convolution fusion | flops 3758096384 | bytes 13893632 | tf_op jit(solution)/shard_map/dot_general | solution.py:63
  (8 shorter events, 0.0 us)
Async XLA Ops:
  7.2 234.5 %all-gather.3.cloned.1.call-start = ((), (), s32[]{:S(2)}) async-start(), calls=%async_computation | async-start | bytes 8912896 | tf_op jit(solution)/shard_map/all_gather | solution.py:62
  10.1 24.2 %collective-permute-start.10 = (f32[1,256,1024]{2,1,0:T(8,128)}, f32[1,256,1024]{2,1,0:T(8,128)S(1)}, u32[]{:S(2)}, u32[]{:S(2)}) collective-permute-start(f32[1,256,1024]{2,1,0:T(8,128)} %get-tuple-element.99), channel_id=1, source_target_pairs={{0,32},{32,0},{16,48},{48,16},{64,96},{96,64},{80,112},{112,80},{1... | collective-permute-start | bytes 3145736 | tf_op jit(solution)/shard_map/cond/branch_1_fun/ppermute | solution.py:25
  10.4 46.5 %collective-permute-start.11 = (f32[1,256,1024]{2,1,0:T(8,128)}, f32[1,256,1024]{2,1,0:T(8,128)S(1)}, u32[]{:S(2)}, u32[]{:S(2)}) collective-permute-start(f32[1,256,1024]{2,1,0:T(8,128)} %get-tuple-element.100), channel_id=1, source_target_pairs={{0,32},{32,0},{16,48},{48,16},{64,96},{96,64},{80,112},{112,80},{1... | collective-permute-start | bytes 3145736 | tf_op jit(solution)/shard_map/cond/branch_1_fun/ppermute | solution.py:25
  34.4 22.5 %copy-start.3 = (f32[1,256,1024]{2,1,0:T(8,128)}, f32[1,256,1024]{2,1,0:T(8,128)S(1)}, u32[]{:S(2)}) copy-start(f32[1,256,1024]{2,1,0:T(8,128)S(1)} %collective-permute-done.10) | copy-start | bytes 3145732 | tf_op jit(solution)/shard_map/cond
  56.8 1.0 copy-start.7
  61.6 24.8 %collective-permute-start.4 = (f32[1,256,1024]{2,1,0:T(8,128)S(1)}, f32[1,256,1024]{2,1,0:T(8,128)}, u32[]{:S(2)}, u32[]{:S(2)}) collective-permute-start(f32[1,256,1024]{2,1,0:T(8,128)S(1)} %get-tuple-element.124), channel_id=1, source_target_pairs={{0,64},{64,0},{16,80},{80,16},{32,96},{96,32},{48,112},{112,48},{1... | collective-permute-start | bytes 3145736 | tf_op jit(solution)/shard_map/cond/branch_2_fun/ppermute | solution.py:25
  63.5 45.4 %collective-permute-start.5 = (f32[1,256,1024]{2,1,0:T(8,128)S(1)}, f32[1,256,1024]{2,1,0:T(8,128)}, u32[]{:S(2)}, u32[]{:S(2)}) collective-permute-start(f32[1,256,1024]{2,1,0:T(8,128)S(1)} %get-tuple-element.127), channel_id=1, source_target_pairs={{0,64},{64,0},{16,80},{80,16},{32,96},{96,32},{48,112},{112,48},{1... | collective-permute-start | bytes 3145736 | tf_op jit(solution)/shard_map/cond/branch_2_fun/ppermute | solution.py:25
  116.1 135.2 %copy-start = (f32[1,256,1024]{2,1,0:T(8,128)}, f32[1,256,1024]{2,1,0:T(8,128)S(1)}, u32[]{:S(2)}) copy-start(f32[1,256,1024]{2,1,0:T(8,128)S(1)} %get-tuple-element.145) | copy-start | bytes 3145732
  116.1 135.2 %copy-start.1 = (f32[1,256,1024]{2,1,0:T(8,128)}, f32[1,256,1024]{2,1,0:T(8,128)S(1)}, u32[]{:S(2)}) copy-start(f32[1,256,1024]{2,1,0:T(8,128)S(1)} %get-tuple-element.146) | copy-start | bytes 3145732
Sparse Core Ops, SparseCore 0:
  120.1 121.5 all-gather.2
where the time goes:
time: 259 us; the launch traced here: 258 us
  waiting for transfers between devices  208 us (80%)
  between operations  14.8 us (6%)
  other arithmetic  12.7 us (5%)
  matrix products  9.68 us (4%)
  local copies, waits for them, and re-layouts  8.09 us (3%)
  starting transfers between devices  4.56 us (2%)
    all_gather x1, waiting for transfers between devices, per_device(): whole = lax.all_gather(rounded, 'fsdp', axis=0, tiled=True)  122 us
    ppermute x4, waiting for transfers between devices, from_partner(): return lax.ppermute(block, axis, route)  86.2 us
    dot_general x1, matrix products, per_device(): total = jnp.dot(rows, whole, preferred_element_type=jnp.float32)  9.68 us
  transfers between devices with their start and end apart: 5, of which 5 were waited for; matrix products, arithmetic and copies ran while one was open for 1% of the time, Pallas kernels for 0%

commit v1 on v0

v1 whole, which is shorter than its diff:
```python
from functools import partial

import jax
import jax.numpy as jnp
from jax import lax
from jax.experimental import pallas as pl
from jax.experimental.pallas import tpu as pltpu
from jax.sharding import PartitionSpec as P

BETA_ONE = 0.9
BETA_TWO = 0.95
RATE = 0.003
DECAY = 0.1
EPSILON = 1e-08

LEVELS = 4
D = 4096
KVW = 1024
ROWS = 256
TOK = 448
R = 128
H = ROWS // R
HALF = R // 2
COLS = 128
NB = KVW // COLS
NC = NB * H
AHEAD = 2
LAG_TWO, LAG_Z1, LAG_Z2, LAG_Y1, LAG_Y1F, LAG_Y2, LAG_END = 1, 2, 3, 3, 4, 4, 5
DEEP = 1024


def adam(w, m, far_w, far_m, v, g, inv_one, inv_two):
    gf = g.astype(jnp.float32)
    avg_w = 0.5 * (w + far_w)
    avg_m = 0.5 * (m + far_m)
    moment = BETA_ONE * avg_m + (1.0 - BETA_ONE) * gf
    second = BETA_TWO * v + (1.0 - BETA_TWO) * gf * gf
    update = (moment * inv_one) / (jnp.sqrt(second * inv_two) + EPSILON) + DECAY * avg_w
    return avg_w - RATE * update, moment, second


def kernel(levels, wide, corr, w, m, v, g, tok, new_w, new_m, new_v, proj,
           wm, vs, gs, toks, rx_one, tx_two, rx_two, gat,
           in_wm, in_v, in_g, in_tok, s_one, s_two, s_gat, r_one, r_two,
           r_z1, r_z2, r_y1, r_y1n, r_y1f, r_y2, r_end):
    gossip = lax.axis_index("gossip")
    me = lax.axis_index("fsdp")
    y, z = me // 4, me % 4

    def at(dy, dz):
        return ((y + dy) % 4) * 4 + (z + dz) % 4

    def partner(level):
        apart = 1 << level
        return gossip + apart * (1 - 2 * ((gossip // apart) % 2))

    first, then = partner(levels[0]), partner(levels[1])
    y_up, y_down, z_up, z_down = at(1, 0), at(3, 0), at(0, 1), at(0, 3)

    def rows_of(c):
        return pl.ds(pl.multiple_of((c % H) * R, R), R)

    def cols_of(c):
        return pl.ds(pl.multiple_of((c // H) * COLS, COLS), COLS)

    def piece(c, owner):
        return gat.at[c // H, pl.ds(pl.multiple_of(owner * ROWS + (c % H) * R, R), R), :]

    def half(c, owner, which):
        start = owner * ROWS + (c % H) * R + which * HALF
        return gat.at[c // H, pl.ds(pl.multiple_of(start, HALF), HALF), :]

    def wait_pieces(c, count, sem):
        ref = gat.at[c // H, pl.ds(0, count * R), :]
        pltpu.make_async_copy(ref, ref, sem.at[c]).wait()

    def wait_for(ref, sem):
        pltpu.make_async_copy(ref, ref, sem).wait()

    def give(ref, c, sem, to):
        pltpu.make_async_remote_copy(
            src_ref=ref, dst_ref=ref, send_sem=s_gat.at[c], recv_sem=sem.at[c],
            device_id={"fsdp": to}, device_id_type=pl.DeviceIdType.MESH).start()

    def fetch(c, _):
        pltpu.make_async_copy(w.at[0, rows_of(c), cols_of(c)], wm.at[c, 0], in_wm.at[c]).start()
        pltpu.make_async_copy(m.at[0, rows_of(c), cols_of(c)], wm.at[c, 1], in_wm.at[c]).start()
        pltpu.make_async_copy(v.at[0, rows_of(c), cols_of(c)], vs.at[c], in_v.at[c]).start()
        pltpu.make_async_copy(g.at[:, 0, rows_of(c), cols_of(c)], gs.at[c], in_g.at[c]).start()
        return 0

    lax.fori_loop(0, NC, fetch, 0)
    pltpu.make_async_copy(tok.at[0], toks, in_tok).start()

    barrier = pltpu.get_barrier_semaphore()
    for other in (first, then):
        pl.semaphore_signal(barrier, inc=1, device_id={"gossip": other}, device_id_type=pl.DeviceIdType.MESH)
    for other in (y_up, y_down, z_up, z_down):
        pl.semaphore_signal(barrier, inc=1, device_id={"fsdp": other}, device_id_type=pl.DeviceIdType.MESH)
    pl.semaphore_wait(barrier, 6)

    def send_one(c):
        wait_for(wm.at[c], in_wm.at[c])
        pltpu.make_async_remote_copy(
            src_ref=wm.at[c], dst_ref=rx_one.at[c], send_sem=s_one.at[c], recv_sem=r_one.at[c],
            device_id={"gossip": first}, device_id_type=pl.DeviceIdType.MESH).start()

    def step_one(c):
        wait_for(vs.at[c], in_v.at[c])
        wait_for(gs.at[c], in_g.at[c])
        wait_for(rx_one.at[c], r_one.at[c])
        nw, nm, nv = adam(wm[c, 0], wm[c, 1], rx_one[c, 0], rx_one[c, 1], vs[c], gs[c, 0], corr[0], corr[1])
        tx_two[c, 0] = nw
        tx_two[c, 1] = nm
        vs[c] = nv
        pltpu.make_async_remote_copy(
            src_ref=tx_two.at[c], dst_ref=rx_two.at[c], send_sem=s_two.at[c], recv_sem=r_two.at[c],
            device_id={"gossip": then}, device_id_type=pl.DeviceIdType.MESH).start()

    def step_two(c):
        wait_for(rx_two.at[c], r_two.at[c])
        nw, nm, nv = adam(tx_two[c, 0], tx_two[c, 1], rx_two[c, 0], rx_two[c, 1], vs[c], gs[c, 1], corr[2], corr[3])
        new_w[0, rows_of(c), cols_of(c)] = nw
        new_m[0, rows_of(c), cols_of(c)] = nm
        new_v[0, rows_of(c), cols_of(c)] = nv
        own = pl.ds(pl.multiple_of(me * ROWS + (c % H) * R, R), R)
        gat[c // H, own, :] = nw.astype(jnp.bfloat16)
        mine = piece(c, me)
        give(mine, c, r_z1, z_up)
        give(mine, c, r_z1, z_down)
        give(mine, c, r_y1, y_up)
        give(mine, c, r_y1, y_down)

    def z_one(c):
        wait_pieces(c, 2, r_z1)
        give(half(c, z_down, 0), c, r_z2, z_up)
        give(half(c, z_up, 1), c, r_z2, z_down)
        for owner in (z_down, z_up):
            give(piece(c, owner), c, r_y1n, y_up)
            give(piece(c, owner), c, r_y1n, y_down)

    def z_two(c):
        wait_pieces(c, 1, r_z2)
        give(piece(c, at(0, 2)), c, r_y1f, y_up)
        give(piece(c, at(0, 2)), c, r_y1f, y_down)

    def y_one(c):
        wait_pieces(c, 2, r_y1)
        give(half(c, at(3, 0), 0), c, r_y2 if wide else r_end, y_up)
        give(half(c, at(1, 0), 1), c, r_y2 if wide else r_end, y_down)
        if not wide:
            wait_pieces(c, 4, r_y1n)
            for dz in (1, 3):
                give(half(c, at(3, dz), 0), c, r_end, y_up)
                give(half(c, at(1, dz), 1), c, r_end, y_down)

    def y_one_far(c):
        wait_pieces(c, 2, r_y1f)
        give(half(c, at(3, 2), 0), c, r_end, y_up)
        give(half(c, at(1, 2), 1), c, r_end, y_down)

    def y_two(c):
        if wide:
            wait_pieces(c, 1, r_y2)
            for which in (0, 1):
                give(half(c, at(2, 0), which), c, r_end, z_up)
                give(half(c, at(2, 0), which), c, r_end, z_down)

    def finish(c):
        if wide:
            wait_pieces(c, 4, r_y1n)
            wait_pieces(c, 3, r_end)
        else:
            wait_pieces(c, 4, r_end)

        @pl.when(c % (2 * H) == 2 * H - 1)
        def _():
            pair = c // (2 * H)

            @pl.when(pair == 0)
            def _():
                wait_for(toks, in_tok)

            out = pl.ds(pl.multiple_of(pair * 2 * COLS, 2 * COLS), 2 * COLS)
            for part in range(D // DEEP):
                deep = pl.ds(part * DEEP, DEEP)
                both = jnp.concatenate([gat[2 * pair, deep, :], gat[2 * pair + 1, deep, :]], axis=1)
                add = jnp.dot(toks[:, deep], both, preferred_element_type=jnp.float32)
                if part == 0:
                    proj[0, :, out] = add
                else:
                    proj[0, :, out] += add

    def start(c, _):
        send_one(c)
        return 0

    lax.fori_loop(0, AHEAD, start, 0)

    stages = ((-AHEAD, send_one), (0, step_one), (LAG_TWO, step_two), (LAG_Z1, z_one), (LAG_Z2, z_two),
              (LAG_Y1, y_one), (LAG_Y1F, y_one_far), (LAG_Y2, y_two), (LAG_END, finish))

    def tick(t, _):
        for lag, stage in stages:
            c = t - lag

            @pl.when((c >= 0) & (c < NC))
            def _(c=c, stage=stage):
                stage(c)

        return 0

    lax.fori_loop(0, NC + LAG_END, tick, 0)

    def drain(c, _):
        wait_for(wm.at[c], s_one.at[c])
        wait_for(tx_two.at[c], s_two.at[c])
        wait_pieces(c, 15, s_gat)
        return 0

    lax.fori_loop(0, NC, drain, 0)


def fused(case, corr, w, m, v, g, tok):
    levels = (case, (case + 1) % LEVELS)
    wide = LEVELS - 1 not in levels
    dma = pltpu.SemaphoreType.DMA
    f32, bf16 = jnp.float32, jnp.bfloat16
    block = jax.ShapeDtypeStruct((1, ROWS, KVW), f32)
    hbm = pl.BlockSpec(memory_space=pl.ANY)
    vmem = pl.BlockSpec(memory_space=pltpu.VMEM)
    return pl.pallas_call(
        partial(kernel, levels, wide),
        out_shape=(block, block, block, jax.ShapeDtypeStruct((1, TOK, KVW), f32)),
        in_specs=[pl.BlockSpec(memory_space=pltpu.SMEM)] + [hbm] * 5,
        out_specs=(vmem,) * 4,
        scratch_shapes=[
            pltpu.VMEM((NC, 2, R, COLS), f32),
            pltpu.VMEM((NC, R, COLS), f32),
            pltpu.VMEM((NC, 2, R, COLS), bf16),
            pltpu.VMEM((TOK, D), bf16),
            pltpu.VMEM((NC, 2, R, COLS), f32),
            pltpu.VMEM((NC, 2, R, COLS), f32),
            pltpu.VMEM((NC, 2, R, COLS), f32),
            pltpu.VMEM((NB, D, COLS), bf16),
            dma((NC,)), dma((NC,)), dma((NC,)), dma,
        ] + [dma((NC,)) for _ in range(12)],
        compiler_params=pltpu.CompilerParams(
            collective_id=case, has_side_effects=True, vmem_limit_bytes=56 * 1024 * 1024),
        name="steps_%d" % case,
    )(corr, w, m, v, g, tok)


def per_device(step_index, weights, momentum, second_moment, gradients, tokens):
    now = step_index[0]
    counts = (now + jnp.arange(1, 3, dtype=jnp.int32)).astype(jnp.float32)
    inv_one = 1.0 / (1.0 - jnp.power(jnp.float32(BETA_ONE), counts))
    inv_two = 1.0 / (1.0 - jnp.power(jnp.float32(BETA_TWO), counts))
    corr = jnp.stack([inv_one[0], inv_two[0], inv_one[1], inv_two[1]])
    return lax.switch(
        jnp.mod(now, LEVELS), [partial(fused, case) for case in range(LEVELS)],
        corr, weights, momentum, second_moment, gradients, tokens)


def solution(mesh):
    split = P("gossip", "fsdp", None)
    return jax.shard_map(
        per_device,
        mesh=mesh,
        in_specs=(P(), split, split, split, P(None, "gossip", "fsdp", None), split),
        out_specs=(split,) * 4,
        check_vma=False,
    )
```

time: 259 us -> 120 us (0.46)
  the two profiles are of different devices: /device:TPU:35 before, /device:TPU:8 now
where the time goes in v1:
time: 120 us; the launch traced here: 119 us
  Pallas kernels  109 us (91%)
  local copies, waits for them, and re-layouts  5.92 us (5%)
  other arithmetic  2.58 us (2%)
  between operations  1.33 us (1%)
    pallas_call x1, Pallas kernels, fused(): pl.pallas_call(partial(kernel, levels, wide), out_shape=(block, block, bl...  109 us
    unnamed x8, local copies, waits for them, and re-layouts  4.76 us
    another operation x1, other arithmetic, per_device(): corr = jnp.stack([inv_one[0], inv_two[0], inv_one[1], inv_two[1]])  2.57 us

profile of v1, /device:TPU:8, one launch (start us, length us, event | category | flops | bytes accessed | tf_op | source)
XLA Modules:
  0.0 118.8 jit_solution(12845019180592743243)
XLA Ops:
  1.3 0.6 fusion.1
  1.9 0.6 fusion
  2.5 2.6 %pad_maximum_fusion = f32[4]{0:T(128)S(1)} fusion(f32[1]{0:T(128)} %get-tuple-element.139, f32[1]{0:T(128)} %get-tuple-element.137, f32[1]{0:T(128)} %get-tuple-element.138, f32[1]{0:T(128)} %get-tuple-element.136), kind=kLoop, calls=%fused_computation | loop fusion | flops 12 | bytes 32 | tf_op jit(solution)/shard_map/stack | solution.py:259
  5.0 109.0 %conditional.1 = ((f32[1,256,1024]{2,1,0:T(8,128)S(1)}, f32[1,256,1024]{2,1,0:T(8,128)}, f32[1,256,1024]{2,1,0:T(8,128)}, f32[1,448,1024]{2,1,0:T(8,128)S(1)})) conditional(s32[]{:T(128)} %clamp.3, (f32[4]{0:T(128)S(1)}, f32[1,256,1024]{2,1,0:T(8,128)}, f32[1,256,1024]{2,1,0:T(8,128)}, f32[1,256,1024]{2,1,0:T(8,128)}, ...), branch_computations={%region_0.1_spmd, %region_1.2_spmd, %region_2.3_spmd, %region_3.4_... | conditional | bytes 8 | solution.py:260
  5.0 109.0 %steps_3.1 = (f32[1,256,1024]{2,1,0:T(8,128)S(1)}, f32[1,256,1024]{2,1,0:T(8,128)}, f32[1,256,1024]{2,1,0:T(8,128)}, f32[1,448,1024]{2,1,0:T(8,128)S(1)}) custom-call(f32[4]{0:T(128)S(1)} %get-tuple-element.66.corr, f32[1,256,1024]{2,1,0:T(8,128)} %get-tuple-element.119.w, f32[1,256,1024]{2,1,0:T(8,128)} %get-tuple-element.123.m, ...), custom_call_target="tpu_custom_call" | custom-call | tf_op jit(solution)/shard_map/cond/branch_3_fun/steps_3/pallas_call | solution.py:232
  114.1 0.0 copy-start
  114.1 0.0 copy-start.1
  114.1 1.0 copy.67
  115.0 0.6 copy-done
  115.7 1.0 copy.68
  116.6 0.0 copy-done.1
  116.6 1.0 copy.69
  117.6 1.2 %copy.70 = f32[1,448,1024]{2,1,0:T(8,128)} copy(f32[1,448,1024]{2,1,0:T(8,128)S(1)} %get-tuple-element.165) | data formatting | bytes 3670016
  (1 shorter events, 0.0 us)
Async XLA Ops:
  114.1 1.6 %copy-start = (f32[1,256,1024]{2,1,0:T(8,128)S(1)}, f32[1,256,1024]{2,1,0:T(8,128)}, u32[]{:S(2)}) copy-start(f32[1,256,1024]{2,1,0:T(8,128)} %get-tuple-element.163) | copy-start | bytes 3145732
  114.1 2.6 %copy-start.1 = (f32[1,256,1024]{2,1,0:T(8,128)S(1)}, f32[1,256,1024]{2,1,0:T(8,128)}, u32[]{:S(2)}) copy-start(f32[1,256,1024]{2,1,0:T(8,128)} %get-tuple-element.164) | copy-start | bytes 3145732

commit v2 on v1

v2 whole, which is shorter than its diff:
```python
from functools import partial

import jax
import jax.numpy as jnp
from jax import lax
from jax.experimental import pallas as pl
from jax.experimental.pallas import tpu as pltpu
from jax.sharding import PartitionSpec as P

BETA_ONE = 0.9
BETA_TWO = 0.95
RATE = 0.003
DECAY = 0.1
EPSILON = 1e-08

LEVELS = 4
D = 4096
KVW = 1024
ROWS = 256
TOK = 448
R = 128
H = ROWS // R
HALF = R // 2
PARTS = R // 8
WORDS = 8 * (1 + PARTS // 2 + PARTS // 8)
STEPS_20 = 524287.0
FINE = 268435456.0
COLS = 128
NB = KVW // COLS
NC = NB * H
PLANS = (
    (7, 2, 4, 6, 4, 10, 8, 14),
    (2, 2, 3, 4, 3, 6, 5, 15),
    (6, 1, 2, 3, 3, 7, 7, 12),
    (2, 1, 2, 3, 3, 7, 4, 11),
)
DEEP = 1024


def adam(w, m, far_w, far_m, v, g, inv_one, inv_two):
    gf = g.astype(jnp.float32)
    avg_w = 0.5 * (w + far_w)
    avg_m = 0.5 * (m + far_m)
    moment = BETA_ONE * avg_m + (1.0 - BETA_ONE) * gf
    second = BETA_TWO * v + (1.0 - BETA_TWO) * gf * gf
    update = (moment * inv_one) / (jnp.sqrt(second * inv_two) + EPSILON) + DECAY * avg_w
    return avg_w - RATE * update, moment, second


def encode(x, put):
    parts = [x[8 * i:8 * i + 8] for i in range(PARTS)]
    top = jnp.abs(parts[0])
    for part in parts[1:]:
        top = jnp.maximum(top, jnp.abs(part))
    top = (top * FINE).astype(jnp.int32) + 1
    put(0, top)
    scale = STEPS_20 / (top.astype(jnp.float32) * (1.0 / FINE))
    whole = [jnp.round(part * scale).astype(jnp.int32) for part in parts]
    for k in range(PARTS // 2):
        put(1 + k, ((whole[2 * k] << 12) & -65536) | ((whole[2 * k + 1] >> 4) & 65535))
    for k in range(PARTS // 8):
        low = whole[8 * k] & 15
        for i in range(1, 8):
            low = low | ((whole[8 * k + i] & 15) << (4 * i))
        put(1 + PARTS // 2 + k, low)


def decode(get):
    scale = (get(0).astype(jnp.float32) * (1.0 / FINE)) * (1.0 / STEPS_20)
    parts = []
    for k in range(PARTS // 2):
        word, low = get(1 + k), get(1 + PARTS // 2 + k // 4)
        shift = 8 * (k % 4)
        first = ((word >> 16) << 4) | ((low >> shift) & 15)
        other = (((word << 16) >> 16) << 4) | ((low >> (shift + 4)) & 15)
        parts += [first.astype(jnp.float32) * scale, other.astype(jnp.float32) * scale]
    return jnp.concatenate(parts, axis=0)


def powers(base, count):
    total, square = jnp.ones(count.shape, jnp.float32), base
    for bit in range(7):
        there = ((count // (1 << bit)) % 2).astype(jnp.float32)
        total = total * (1.0 + there * (square - 1.0))
        square = square * square
    return total


def kernel(levels, wide, plan, step, w, m, v, g, tok, new_w, new_m, new_v, proj,
           gs, toks, tx_one, rx_one, tx_two, rx_two, gat,
           in_sem, s_one, s_two, s_gat, r_one, r_two,
           r_z1, r_z2, r_y1, r_y1n, r_y1f, r_y2, r_end, r_end2):
    gossip = lax.axis_index("gossip")
    me = lax.axis_index("fsdp")
    y, z = me // 4, me % 4

    def at(dy, dz):
        return ((y + dy) % 4) * 4 + (z + dz) % 4

    def partner(level):
        apart = 1 << level
        return gossip + apart * (1 - 2 * ((gossip // apart) % 2))

    first, then = partner(levels[0]), partner(levels[1])
    y_up, y_down, z_up, z_down = at(1, 0), at(3, 0), at(0, 1), at(0, 3)

    def rows_of(c):
        return pl.ds(pl.multiple_of((c % H) * R, R), R)

    def cols_of(c):
        return pl.ds(pl.multiple_of((c // H) * COLS, COLS), COLS)

    def half_rows(c, which):
        return pl.ds(pl.multiple_of((c % H) * R + which * HALF, HALF), HALF)

    def piece(c, dy, dz, rows):
        there = (z + dz) % 4
        return gat.at[c // H, (y + dy) % 4, there // 2, there % 2, rows, :]

    def two_pieces(c, dy, dz, rows):
        return gat.at[c // H, (y + dy) % 4, :, (z + dz) % 2, rows, :]

    def wait_pieces(c, count, sem):
        ref = gat.at[c // H, pl.ds(0, count // 4), :, :, pl.ds(0, R), :]
        if count < 4:
            ref = gat.at[c // H, 0, 0, 0, pl.ds(0, count * R), :] if count * R <= ROWS else (
                gat.at[c // H, 0, pl.ds(0, 1), :, pl.ds(0, R), :])
        pltpu.make_async_copy(ref, ref, sem.at[c]).wait()

    def wait_for(ref, sem):
        pltpu.make_async_copy(ref, ref, sem).wait()

    def give(ref, c, sem, to):
        pltpu.make_async_remote_copy(
            src_ref=ref, dst_ref=ref, send_sem=s_gat.at[c], recv_sem=sem.at[c],
            device_id={"fsdp": to}, device_id_type=pl.DeviceIdType.MESH).start()

    barrier = pltpu.get_barrier_semaphore()
    for other in (first, then):
        pl.semaphore_signal(barrier, inc=1, device_id={"gossip": other}, device_id_type=pl.DeviceIdType.MESH)
    for other in (y_up, y_down, z_up, z_down):
        pl.semaphore_signal(barrier, inc=1, device_id={"fsdp": other}, device_id_type=pl.DeviceIdType.MESH)

    fetches = [pltpu.make_async_copy(src, dst, in_sem.at[i]) for i, (src, dst) in enumerate((
        (w, new_w), (m, new_m), (v, new_v), (g.at[:, 0], gs), (tok.at[0], toks)))]
    for fetch in fetches:
        fetch.start()

    inv_one, inv_two = [], []
    for ahead in (1, 2):
        count = jnp.full((1, COLS), step[0] + ahead, jnp.int32)
        inv_one.append(1.0 / (1.0 - powers(BETA_ONE, count)))
        inv_two.append(1.0 / (1.0 - powers(BETA_TWO, count)))

    def code(c, tx, which, ref):
        def put(k, word):
            tx[c, which, 8 * k:8 * k + 8, :] = word

        encode(ref[0, rows_of(c), cols_of(c)], put)

    def uncode(c, rx, which):
        return decode(lambda k: rx[c, which, 8 * k:8 * k + 8, :])

    def code_both(c, tx):
        code(c, tx, 0, new_w)
        code(c, tx, 1, new_m)

    def exchange(c, tx, rx, send, recv, to):
        pltpu.make_async_remote_copy(
            src_ref=tx.at[c], dst_ref=rx.at[c], send_sem=send.at[c], recv_sem=recv.at[c],
            device_id={"gossip": to}, device_id_type=pl.DeviceIdType.MESH).start()

    def send_one(c):
        code_both(c, tx_one)
        exchange(c, tx_one, rx_one, s_one, r_one, first)

    def update(c, rx, which):
        rows, cols = rows_of(c), cols_of(c)
        nw, nm, nv = adam(new_w[0, rows, cols], new_m[0, rows, cols], uncode(c, rx, 0), uncode(c, rx, 1),
                          new_v[0, rows, cols], gs[which, rows, cols], inv_one[which], inv_two[which])
        new_w[0, rows, cols] = nw
        new_m[0, rows, cols] = nm
        new_v[0, rows, cols] = nv
        return nw

    def step_one(c):
        wait_for(rx_one.at[c], r_one.at[c])
        update(c, rx_one, 0)
        code_both(c, tx_two)
        exchange(c, tx_two, rx_two, s_two, r_two, then)

    def step_two(c):
        wait_for(rx_two.at[c], r_two.at[c])
        nw = update(c, rx_two, 1)
        gat[c // H, y, z // 2, z % 2, rows_of(c), :] = nw.astype(jnp.bfloat16)
        mine = piece(c, 0, 0, rows_of(c))
        give(mine, c, r_z1, z_up)
        give(mine, c, r_z1, z_down)
        give(mine, c, r_y1, y_up)
        give(mine, c, r_y1, y_down)

    def z_one(c):
        wait_pieces(c, 2, r_z1)
        give(piece(c, 0, 3, half_rows(c, 0)), c, r_z2, z_up)
        give(piece(c, 0, 1, half_rows(c, 1)), c, r_z2, z_down)
        both = two_pieces(c, 0, 1, rows_of(c))
        give(both, c, r_y1n, y_up)
        give(both, c, r_y1n, y_down)

    def z_two(c):
        wait_pieces(c, 1, r_z2)
        far = piece(c, 0, 2, rows_of(c))
        give(far, c, r_y1f, y_up)
        give(far, c, r_y1f, y_down)

    def y_one(c):
        wait_pieces(c, 2, r_y1)
        on = r_y2 if wide else r_end
        give(piece(c, 3, 0, half_rows(c, 0)), c, on, y_up)
        give(piece(c, 1, 0, half_rows(c, 1)), c, on, y_down)
        if not wide:
            wait_pieces(c, 4, r_y1n)
            give(two_pieces(c, 3, 1, half_rows(c, 0)), c, r_end, y_up)
            give(two_pieces(c, 1, 1, half_rows(c, 1)), c, r_end, y_down)

    def y_far(c):
        wait_pieces(c, 2, r_y1f)
        last = r_end2 if wide else r_end
        give(piece(c, 3, 2, half_rows(c, 0)), c, last, y_up)
        give(piece(c, 1, 2, half_rows(c, 1)), c, last, y_down)

    def y_two(c):
        wait_pieces(c, 1, r_y2)
        over = piece(c, 2, 0, rows_of(c))
        give(over, c, r_end, z_up)
        give(over, c, r_end, z_down)

    def finish(c):
        if wide:
            wait_pieces(c, 4, r_y1n)
            wait_pieces(c, 1, r_end2)
            wait_pieces(c, 2, r_end)
        else:
            wait_pieces(c, 4, r_end)
        wait_for(tx_one.at[c], s_one.at[c])
        wait_for(tx_two.at[c], s_two.at[c])
        wait_for(gat.at[c // H, :, :, 0, pl.ds(0, 15 * R // 8), :], s_gat.at[c])

        @pl.when(c % (2 * H) == 2 * H - 1)
        def _():
            pair = c // (2 * H)

            @pl.when(pair == 0)
            def _():
                fetches[4].wait()

            out = pl.ds(pl.multiple_of(pair * 2 * COLS, 2 * COLS), 2 * COLS)
            for part in range(4):
                both = jnp.concatenate(
                    [gat[2 * pair + k, part].reshape(DEEP, COLS) for k in (0, 1)], axis=1)
                add = jnp.dot(toks[:, part * DEEP:(part + 1) * DEEP], both, preferred_element_type=jnp.float32)
                if part == 0:
                    proj[0, :, out] = add
                else:
                    proj[0, :, out] += add

    fetches[0].wait()
    fetches[1].wait()
    code_both(0, tx_one)
    pl.semaphore_wait(barrier, 6)
    exchange(0, tx_one, rx_one, s_one, r_one, first)

    def start(c, _):
        send_one(c)
        return 0

    lax.fori_loop(1, plan[0], start, 0)
    fetches[2].wait()
    fetches[3].wait()

    stages = [(-plan[0], send_one), (0, step_one)] + [
        (lag, stage) for lag, stage in zip(plan[1:], (step_two, z_one, z_two, y_one, y_far, y_two, finish))
        if wide or stage is not y_two]

    def tick(t, _):
        for lag, stage in stages:
            c = t - lag

            @pl.when((c >= 0) & (c < NC))
            def _(c=c, stage=stage):
                stage(c)

        return 0

    lax.fori_loop(0, NC + plan[7], tick, 0)


def fused(case, step, w, m, v, g, tok):
    levels = (case, (case + 1) % LEVELS)
    wide = LEVELS - 1 not in levels
    dma = pltpu.SemaphoreType.DMA
    f32, bf16 = jnp.float32, jnp.bfloat16
    block = jax.ShapeDtypeStruct((1, ROWS, KVW), f32)
    hbm = pl.BlockSpec(memory_space=pl.ANY)
    vmem = pl.BlockSpec(memory_space=pltpu.VMEM)
    return pl.pallas_call(
        partial(kernel, levels, wide, PLANS[case]),
        out_shape=(block, block, block, jax.ShapeDtypeStruct((1, TOK, KVW), f32)),
        in_specs=[pl.BlockSpec(memory_space=pltpu.SMEM)] + [hbm] * 5,
        out_specs=(vmem,) * 4,
        scratch_shapes=[
            pltpu.VMEM((2, ROWS, KVW), bf16),
            pltpu.VMEM((TOK, D), bf16),
            pltpu.VMEM((NC, 2, WORDS, COLS), jnp.int32),
            pltpu.VMEM((NC, 2, WORDS, COLS), jnp.int32),
            pltpu.VMEM((NC, 2, WORDS, COLS), jnp.int32),
            pltpu.VMEM((NC, 2, WORDS, COLS), jnp.int32),
            pltpu.VMEM((NB, 4, 2, 2, ROWS, COLS), bf16),
            dma((5,)),
        ] + [dma((NC,)) for _ in range(13)],
        compiler_params=pltpu.CompilerParams(
            collective_id=case, has_side_effects=True, vmem_limit_bytes=56 * 1024 * 1024),
        name="steps_%d" % case,
    )(step, w, m, v, g, tok)


def per_device(step_index, weights, momentum, second_moment, gradients, tokens):
    outs = lax.switch(
        jnp.mod(step_index[0], LEVELS), [partial(fused, case) for case in range(LEVELS)],
        step_index, weights, momentum, second_moment, gradients, tokens)
    return pl.pallas_call(
        put_out,
        out_shape=tuple(jax.ShapeDtypeStruct(o.shape, o.dtype) for o in outs),
        in_specs=[pl.BlockSpec(memory_space=pltpu.VMEM)] * 4,
        out_specs=(pl.BlockSpec(memory_space=pl.ANY),) * 4,
        scratch_shapes=[pltpu.SemaphoreType.DMA((4,))],
        name="put_out",
    )(*outs)


def put_out(*refs):
    sems = refs[8]
    copies = [pltpu.make_async_copy(refs[i], refs[4 + i], sems.at[i]) for i in range(4)]
    for copy in copies:
        copy.start()
    for copy in copies:
        copy.wait()


def solution(mesh):
    split = P("gossip", "fsdp", None)
    return jax.shard_map(
        per_device,
        mesh=mesh,
        in_specs=(P(), split, split, split, P(None, "gossip", "fsdp", None), split),
        out_specs=(split,) * 4,
        check_vma=False,
    )
```

time: 120 us -> 103 us (0.86); the launches traced: 119 us -> 103 us
  Pallas kernels: 109 us -> 102 us
  local copies, waits for them, and re-layouts: 5.92 us -> 0 us
  other arithmetic: 2.58 us -> 0 us
    pallas_call x1 -> x2, Pallas kernels: 109 us -> 102 us  [the longest x1 98 us: fused(): pl.pallas_call(partial(kernel, levels, wide, PLANS[case]), out_shape=(blo...]
    unnamed x8 -> x0, local copies, waits for them, and re-layouts: 4.76 us -> none
    another operation x1 -> x0, other arithmetic: 2.57 us -> none  [per_device(): corr = jnp.stack([inv_one[0], inv_two[0], inv_one[1], inv_two[1]])]
where the time goes in v2:
time: 103 us
  Pallas kernels  102 us (99%)
  between operations  1.3 us (1%)
    pallas_call x1, Pallas kernels, fused(): pl.pallas_call(partial(kernel, levels, wide, PLANS[case]), out_shape=(blo...  98 us
    pallas_call x1, Pallas kernels, per_device(): pl.pallas_call(put_out, out_shape=tuple((jax.ShapeDtypeStruct(o.shape, o....  3.84 us

profile of v2, /device:TPU:8, one launch (start us, length us, event | category | flops | bytes accessed | tf_op | source)
XLA Modules:
  0.0 103.2 jit_solution(15863167760260606227)
XLA Ops:
  1.3 98.1 %conditional.1 = ((f32[1,256,1024]{2,1,0:T(8,128)S(1)}, f32[1,256,1024]{2,1,0:T(8,128)}, f32[1,256,1024]{2,1,0:T(8,128)}, f32[1,448,1024]{2,1,0:T(8,128)S(1)})) conditional(s32[]{:T(128)} %clamp.3, (s32[1]{0:T(128)}, f32[1,256,1024]{2,1,0:T(8,128)}, f32[1,256,1024]{2,1,0:T(8,128)}, f32[1,256,1024]{2,1,0:T(8,128)}, ...), branch_computations={%region_0.1_spmd, %region_1.2_spmd, %region_2.3_spmd, %region_3.4_... | conditional | bytes 8 | solution.py:328
  1.3 98.0 %steps_2.1 = (f32[1,256,1024]{2,1,0:T(8,128)S(1)}, f32[1,256,1024]{2,1,0:T(8,128)}, f32[1,256,1024]{2,1,0:T(8,128)}, f32[1,448,1024]{2,1,0:T(8,128)S(1)}) custom-call(s32[1]{0:T(128)} %get-tuple-element.60.step, f32[1,256,1024]{2,1,0:T(8,128)} %get-tuple-element.61.w, f32[1,256,1024]{2,1,0:T(8,128)} %get-tuple-element.62.m, ...), custom_call_target="tpu_custom_call" | custom-call | tf_op jit(solution)/shard_map/cond/branch_2_fun/steps_2/pallas_call | solution.py:306
  99.4 3.8 %put_out.1 = (f32[1,256,1024]{2,1,0:T(8,128)}, f32[1,256,1024]{2,1,0:T(8,128)}, f32[1,256,1024]{2,1,0:T(8,128)}, f32[1,448,1024]{2,1,0:T(8,128)}) custom-call(f32[1,256,1024]{2,1,0:T(8,128)S(1)} %get-tuple-element.80.refs_0_, f32[1,256,1024]{2,1,0:T(8,128)} %get-tuple-element.81.refs_1_, f32[1,256,1024]{2,1,0:T(8,128)} %get-tuple-element.82.refs_2_, ...), custom_call_target="tpu_custom_call" | custom-call | tf_op jit(solution)/shard_map/put_out/pallas_call | solution.py:331

commit v3 on v2

--- a/solution.py
+++ b/solution.py
@@ -22,8 +22,8 @@
 H = ROWS // R
 HALF = R // 2
 PARTS = R // 8
-WORDS = 8 * (1 + PARTS // 2 + PARTS // 8)
-STEPS_20 = 524287.0
+WORDS = 8 * (1 + PARTS // 2 + PARTS // 16)
+STEPS_18 = 131071.0
 FINE = 268435456.0
 COLS = 128
 NB = KVW // COLS
@@ -54,25 +54,25 @@
         top = jnp.maximum(top, jnp.abs(part))
     top = (top * FINE).astype(jnp.int32) + 1
     put(0, top)
-    scale = STEPS_20 / (top.astype(jnp.float32) * (1.0 / FINE))
+    scale = STEPS_18 / (top.astype(jnp.float32) * (1.0 / FINE))
     whole = [jnp.round(part * scale).astype(jnp.int32) for part in parts]
     for k in range(PARTS // 2):
-        put(1 + k, ((whole[2 * k] << 12) & -65536) | ((whole[2 * k + 1] >> 4) & 65535))
-    for k in range(PARTS // 8):
-        low = whole[8 * k] & 15
-        for i in range(1, 8):
-            low = low | ((whole[8 * k + i] & 15) << (4 * i))
+        put(1 + k, ((whole[2 * k] << 14) & -65536) | ((whole[2 * k + 1] >> 2) & 65535))
+    for k in range(PARTS // 16):
+        low = whole[16 * k] & 3
+        for i in range(1, 16):
+            low = low | ((whole[16 * k + i] & 3) << (2 * i))
         put(1 + PARTS // 2 + k, low)
 
 
 def decode(get):
-    scale = (get(0).astype(jnp.float32) * (1.0 / FINE)) * (1.0 / STEPS_20)
+    scale = (get(0).astype(jnp.float32) * (1.0 / FINE)) * (1.0 / STEPS_18)
     parts = []
     for k in range(PARTS // 2):
-        word, low = get(1 + k), get(1 + PARTS // 2 + k // 4)
-        shift = 8 * (k % 4)
-        first = ((word >> 16) << 4) | ((low >> shift) & 15)
-        other = (((word << 16) >> 16) << 4) | ((low >> (shift + 4)) & 15)
+        word, low = get(1 + k), get(1 + PARTS // 2 + k // 8)
+        shift = 4 * (k % 8)
+        first = ((word >> 16) << 2) | ((low >> shift) & 3)
+        other = (((word << 16) >> 16) << 2) | ((low >> (shift + 2)) & 3)
         parts += [first.astype(jnp.float32) * scale, other.astype(jnp.float32) * scale]
     return jnp.concatenate(parts, axis=0)
 
@@ -319,7 +319,7 @@
             dma((5,)),
         ] + [dma((NC,)) for _ in range(13)],
         compiler_params=pltpu.CompilerParams(
-            collective_id=case, has_side_effects=True, vmem_limit_bytes=56 * 1024 * 1024),
+            collective_id=case, has_side_effects=True, vmem_limit_bytes=40 * 1024 * 1024),
         name="steps_%d" % case,
     )(step, w, m, v, g, tok)
 
@@ -334,6 +334,7 @@
         in_specs=[pl.BlockSpec(memory_space=pltpu.VMEM)] * 4,
         out_specs=(pl.BlockSpec(memory_space=pl.ANY),) * 4,
         scratch_shapes=[pltpu.SemaphoreType.DMA((4,))],
+        compiler_params=pltpu.CompilerParams(vmem_limit_bytes=8 * 1024 * 1024),
         name="put_out",
     )(*outs)
 

time: 103 us -> 103 us (level); the launches traced: 103 us -> 102 us
    pallas_call x1, Pallas kernels: 98 us -> 97 us  [fused(): pl.pallas_call(partial(kernel, levels, wide, PLANS[case]), out_shape=(blo...]
where the time goes in v3:
time: 103 us; the launch traced here: 102 us
  Pallas kernels  101 us (98%)
  between operations  1.3 us (1%)
    pallas_call x1, Pallas kernels, fused(): pl.pallas_call(partial(kernel, levels, wide, PLANS[case]), out_shape=(blo...  97 us
    pallas_call x1, Pallas kernels, per_device(): pl.pallas_call(put_out, out_shape=tuple((jax.ShapeDtypeStruct(o.shape, o....  3.84 us

profile of v3, /device:TPU:8, one launch (start us, length us, event | category | flops | bytes accessed | tf_op | source)
XLA Modules:
  0.0 102.2 jit_solution(152842374618016858)
XLA Ops:
  1.3 97.0 %conditional.1 = ((f32[1,256,1024]{2,1,0:T(8,128)S(1)}, f32[1,256,1024]{2,1,0:T(8,128)}, f32[1,256,1024]{2,1,0:T(8,128)}, f32[1,448,1024]{2,1,0:T(8,128)S(1)})) conditional(s32[]{:T(128)} %clamp.3, (s32[1]{0:T(128)}, f32[1,256,1024]{2,1,0:T(8,128)}, f32[1,256,1024]{2,1,0:T(8,128)}, f32[1,256,1024]{2,1,0:T(8,128)}, ...), branch_computations={%region_0.1_spmd, %region_1.2_spmd, %region_2.3_spmd, %region_3.4_... | conditional | bytes 8 | solution.py:328
  1.3 97.0 %steps_2.1 = (f32[1,256,1024]{2,1,0:T(8,128)S(1)}, f32[1,256,1024]{2,1,0:T(8,128)}, f32[1,256,1024]{2,1,0:T(8,128)}, f32[1,448,1024]{2,1,0:T(8,128)S(1)}) custom-call(s32[1]{0:T(128)} %get-tuple-element.60.step, f32[1,256,1024]{2,1,0:T(8,128)} %get-tuple-element.61.w, f32[1,256,1024]{2,1,0:T(8,128)} %get-tuple-element.62.m, ...), custom_call_target="tpu_custom_call" | custom-call | tf_op jit(solution)/shard_map/cond/branch_2_fun/steps_2/pallas_call | solution.py:306
  98.3 3.8 %put_out.1 = (f32[1,256,1024]{2,1,0:T(8,128)}, f32[1,256,1024]{2,1,0:T(8,128)}, f32[1,256,1024]{2,1,0:T(8,128)}, f32[1,448,1024]{2,1,0:T(8,128)}) custom-call(f32[1,256,1024]{2,1,0:T(8,128)S(1)} %get-tuple-element.80.refs_0_, f32[1,256,1024]{2,1,0:T(8,128)} %get-tuple-element.81.refs_1_, f32[1,256,1024]{2,1,0:T(8,128)} %get-tuple-element.82.refs_2_, ...), custom_call_target="tpu_custom_call" | custom-call | tf_op jit(solution)/shard_map/put_out/pallas_call | solution.py:331
